TPU v7x, 256 devices: a whole 4x4x8 slice. The times are simulated.
256 devices in a mesh: grp: 2 (over core), dev: 128 (over x, z, y).
Axes of the slice: x: 4, y: 4, z: 8, core: 2. Of those that a mesh axis runs over, the one named last changes fastest.
Arguments:
- teacher_input: bfloat16 [32768, 2048], P(('grp', 'dev')), may hold values from -6 to 6
- expert_routes: int32 [32768, 8], P(('grp', 'dev')), may hold values from 0 to 127, all different within a row; in each aligned block of 128 rows (0 to 127, 128 to 255, ...) at most 12 rows name the same one
- route_gates: float32 [32768, 8], P(('grp', 'dev')), may hold values from 0.05 to 0.3
- expert_gate_up: bfloat16 [128, 2048, 1536], P('dev'), may hold values from -0.125 to 0.125
- expert_down: bfloat16 [128, 768, 1024], P('dev'), may hold values from -0.21875 to 0.21875
- student_owner: int32 [32768], P(('grp', 'dev')), may hold values from 0 to 127, as said below
- student_input: bfloat16 [32768, 1792], P(('grp', 'dev')), may hold values from -24 to 24
- student_gain: float32 [1792], replicated, may hold values from 0.5 to 1.5
- align_weight: bfloat16 [1792, 1024], P('dev'), may hold values from -0.125 to 0.125
Outputs:
- token_loss: float32 [32768], P(('grp', 'dev'))
- input_grad: bfloat16 [32768, 1792], P(('grp', 'dev'))
- gain_grad: float32 [1792], replicated
- align_grad: float32 [1792, 1024], P('dev')
Inputs may be any that keep to these rules, and one draw needn't show every extreme that they name: `expert_routes`: in each aligned block of 128 rows (the rows of one device) no expert is named by more than 12 routes, a bound that some block reaches; a row's 8 experts differ. `student_owner`: the 128 tokens of each device name every owner exactly 1 times; the owner is a device of the token's own half along grp.
All inputs are finite; a program needn't handle non-finite values.
Results may differ from a plain program's by a relative error of at most 0.013.
Values may be sent and summed in bfloat16 or wider, within the bound.
No kernel may reach another device: no remote copies, remote signals or barrier semaphores. Data moves between devices by JAX's collectives and lax.ppermute only.
A program may use at most 128 MiB of HBM per device.

v0:
```python
import math

import jax
import jax.numpy as jnp
from jax import lax
from jax.sharding import PartitionSpec as P

epsilon = 1e-06


def expert_rows(inputs, gate_up, down_proj):
    hidden_both = jnp.dot(inputs, gate_up, preferred_element_type=jnp.float32)
    split_at = gate_up.shape[1] // 2
    hidden = (jax.nn.silu(hidden_both[:, :split_at]) * hidden_both[:, split_at:]).astype(
        jnp.bfloat16
    )
    return jnp.dot(hidden, down_proj, preferred_element_type=jnp.float32).astype(jnp.bfloat16)


def row_scale(values):
    return lax.rsqrt(jnp.mean(values * values, axis=-1, keepdims=True) + epsilon)


def rank_within(labels, label_count):
    label_hot = (labels[:, None] == jnp.arange(label_count, dtype=jnp.int32)[None, :]).astype(
        jnp.int32
    )
    earlier = jnp.cumsum(label_hot, axis=0) - label_hot
    return jnp.sum(earlier * label_hot, axis=1)


def body(
    teacher_input,
    expert_routes,
    route_gates,
    expert_gate_up,
    expert_down,
    student_owner,
    student_input,
    student_gain,
    align_weight,
):
    tok_rows = teacher_input.shape[0]
    top_count = expert_routes.shape[1]
    width_in = teacher_input.shape[1]
    owner_count = lax.axis_size("dev")
    capacity = 3 * tok_rows * top_count // (2 * owner_count)
    pair_count = tok_rows * top_count
    flat_routes = expert_routes.reshape(-1)
    route_slot = rank_within(flat_routes, owner_count)
    slot_place = flat_routes * capacity + route_slot
    slot_table = (
        jnp.full((owner_count * capacity,), pair_count, jnp.int32)
        .at[slot_place]
        .set(jnp.arange(pair_count, dtype=jnp.int32))
    )
    padded = jnp.concatenate([teacher_input, jnp.zeros((1, width_in), teacher_input.dtype)], axis=0)
    source_rows = jnp.where(slot_table < pair_count, slot_table // top_count, tok_rows)
    outgoing = padded[source_rows].reshape(owner_count, capacity, width_in)
    gate_up = expert_gate_up[0]
    down_proj = expert_down[0]
    arrived = lax.all_to_all(outgoing, "dev", split_axis=0, concat_axis=0, tiled=True)
    senders = arrived.shape[0]
    slot_count = arrived.shape[1]
    produced = expert_rows(arrived.reshape(senders * slot_count, width_in), gate_up, down_proj)
    produced = produced.reshape(senders, slot_count, down_proj.shape[1])
    returned = lax.all_to_all(produced, "dev", split_axis=0, concat_axis=0, tiled=True)
    picked = returned.reshape(owner_count * capacity, -1)[slot_place].reshape(
        tok_rows, top_count, -1
    )
    teacher_out = jnp.einsum("tk,tkd->td", route_gates, picked.astype(jnp.float32))
    teacher_target = (teacher_out * row_scale(teacher_out)).astype(jnp.bfloat16)
    per_owner = tok_rows // owner_count
    owner_place = student_owner * per_owner + rank_within(student_owner, owner_count)
    inverse = (
        jnp.zeros((tok_rows,), jnp.int32).at[owner_place].set(jnp.arange(tok_rows, dtype=jnp.int32))
    )
    relay_rows = teacher_target[inverse].reshape(owner_count, per_owner, -1)
    student_target = lax.all_to_all(
        relay_rows, "dev", split_axis=0, concat_axis=0, tiled=True
    ).reshape(tok_rows, -1)
    full_weight = lax.all_gather(align_weight, "dev", axis=0, tiled=True)
    inputs_f = student_input.astype(jnp.float32)
    scale_rows = row_scale(inputs_f)
    unit_rows = inputs_f * scale_rows
    normed = (unit_rows * student_gain).astype(jnp.bfloat16)
    student_out = jnp.dot(normed, full_weight, preferred_element_type=jnp.float32)
    distance = student_out - student_target.astype(jnp.float32)
    token_loss = jnp.mean(distance * distance, axis=-1)
    distance_bf = distance.astype(jnp.bfloat16)
    normed_grad = lax.dot_general(
        distance_bf, full_weight, (((1,), (1,)), ((), ())), preferred_element_type=jnp.float32
    )
    gain_inner = normed_grad * student_gain
    input_grad = (
        scale_rows
        * (gain_inner - unit_rows * jnp.mean(gain_inner * unit_rows, axis=-1, keepdims=True))
    ).astype(jnp.bfloat16)
    tokens_all = tok_rows * lax.axis_size("grp") * owner_count
    grad_factor = 1.0 / math.sqrt(tokens_all)
    gain_grad = lax.psum(jnp.sum(normed_grad * unit_rows, axis=0), ("grp", "dev")) * grad_factor
    whole_term = lax.dot_general(
        normed, distance_bf, (((0,), (0,)), ((), ())), preferred_element_type=jnp.float32
    )
    summed = lax.psum(whole_term.astype(jnp.bfloat16), "grp").astype(jnp.float32)
    shard_part = lax.psum_scatter(summed, "dev", scatter_dimension=0, tiled=True)
    align_grad = shard_part * grad_factor
    return (token_loss, input_grad, gain_grad, align_grad)


def solution(mesh):
    placed = (
        P(("grp", "dev"), None),
        P(("grp", "dev"), None),
        P(("grp", "dev"), None),
        P("dev", None, None),
        P("dev", None, None),
        P(("grp", "dev")),
        P(("grp", "dev"), None),
        P(),
        P("dev", None),
    )
    return jax.shard_map(
        body,
        mesh=mesh,
        in_specs=placed,
        out_specs=(P(("grp", "dev")), P(("grp", "dev"), None), P(), P("dev", None)),
        check_vma=False,
    )
```

profile of v0, /device:TPU:1, one launch (start us, length us, event | category | flops | bytes accessed | tf_op | source)
XLA Modules:
  0.0 1015.6 jit_solution(4335077759958329141)
XLA Ops:
  7.2 0.9 copy.19
  8.3 0.7 broadcast_multiply_fusion.1
  9.1 0.2 fusion.23
  9.7 0.4 fusion.20
  10.1 4.3 scatter_custom_fusion
  14.4 1.1 concatenate.3
  15.5 7.1 gather_fusion
  22.6 10.6 %reshape.98 = bf16[128,12,2048]{2,1,0:T(8,128)(2,1)} reshape(bf16[1536,2048]{1,0:T(8,128)(2,1)} %gather_fusion) | data formatting | bytes 12582912 | tf_op jit(solution)/shard_map/reshape | solution.py:59
  33.2 199.5 %all_to_all.15 = bf16[128,12,2048]{2,1,0:T(8,128)(2,1)} all-to-all(bf16[128,12,2048]{2,1,0:T(8,128)(2,1)} %reshape.98), channel_id=1, replica_groups=mesh['grp'=2,'dev'=128] {'dev'}, dimensions={0} | all-to-all | bytes 12582912 | tf_op jit(solution)/shard_map/all_to_all | solution.py:62
  232.7 10.7 %reshape.99 = bf16[1536,2048]{1,0:T(8,128)(2,1)} reshape(bf16[128,12,2048]{2,1,0:T(8,128)(2,1)} %all_to_all.15) | data formatting | bytes 12582912 | tf_op jit(solution)/shard_map/reshape | solution.py:65
  243.4 14.1 %fusion.1 = f32[1536,1536]{1,0:T(8,128)S(1)} fusion(bf16[1536,2048]{1,0:T(8,128)(2,1)} %reshape.99, bf16[1,2048,1536]{2,1,0:T(8,128)(2,1)} %param.12), kind=kOutput, calls=%fused_computation.5 | convolution fusion | flops 9663676416 | bytes 22020096 | tf_op jit(solution)/shard_map/dot_general | solution.py:12
  257.5 4.0 convolution_convert_fusion.1
  261.5 6.1 reshape.100
  267.6 11.5 %all-to-all-start.1 = ((bf16[128,12,1024]{2,1,0:T(8,128)(2,1)}), bf16[128,12,1024]{2,1,0:T(8,128)(2,1)}, u32[]{:S(2)}, u32[]{:S(2)}) async-start(bf16[128,12,1024]{2,1,0:T(8,128)(2,1)} %reshape.100), calls=%async_computation.1 | async-start | bytes 8388608 | tf_op jit(solution)/shard_map/all_to_all | solution.py:67
  279.1 0.7 all-gather.3.cloned.1.call-update
  280.1 0.2 reduce_window_sum.28
  280.3 0.2 select_reduce_fusion
  280.5 1.0 scatter_custom_fusion.1
  281.5 94.5 %all-to-all-done.1 = bf16[128,12,1024]{2,1,0:T(8,128)(2,1)} async-done(((bf16[128,12,1024]{2,1,0:T(8,128)(2,1)}), bf16[128,12,1024]{2,1,0:T(8,128)(2,1)}, u32[]{:S(2)}, u32[]{:S(2)}) %all-to-all-start.1) | async-done | bytes 3145760 | tf_op jit(solution)/shard_map/all_to_all | solution.py:67
  376.0 4.7 reshape.101
  380.7 5.4 gather_fusion.1
  386.1 2.4 fusion.5
  388.5 0.2 fusion.21
  388.6 0.2 fusion.22
  388.8 0.9 gather_fusion.2
  389.7 0.5 broadcast.145
  390.2 0.8 reduce
  391.0 0.9 reshape.157
  391.9 10.6 %all-to-all-start.2 = ((bf16[128,2,512]{2,1,0:T(2,128)(2,1)}), bf16[128,2,512]{2,1,0:T(2,128)(2,1)S(1)}, u32[]{:S(2)}, u32[]{:S(2)}) async-start(bf16[128,2,512]{2,1,0:T(2,128)(2,1)} %reshape.157), calls=%async_computation.2 | async-start | bytes 524288 | tf_op jit(solution)/shard_map/all_to_all | solution.py:79
  402.5 0.2 fusion.18
  402.7 7.6 all-gather.3.cloned.1.call-done
  410.4 6.5 reshape.149
  416.8 0.2 reshape.158
  417.1 2.9 multiply_reduce_fusion
  420.0 3.0 convolution_convert_fusion
  423.0 0.6 dynamic-slice.4
  424.3 3.5 fusion.17
  427.8 31.7 %all-reduce.5.cloned.1.call-done = bf16[1792,1024]{1,0:T(8,128)(2,1)} async-done(((bf16[1792,1024]{1,0:T(8,128)(2,1)}), bf16[1792,1024]{1,0:T(8,128)(2,1)}) %all-reduce.5.cloned.1.call-update) | async-done | bytes 3670032 | tf_op jit(solution)/shard_map/psum | solution.py:105
  459.5 6.0 convert_element_type.57
  465.5 346.3 %fusion = f32[16,1024]{1,0:T(8,128)S(1)} fusion(f32[1792,1024]{1,0:T(8,128)} %convert_element_type.57), kind=kCustom, calls=%all-reduce-scatter | all-reduce-scatter fusion | flops 2097153 | bytes 7406592
  811.8 1.3 collective-permute-start.15
  813.1 1.3 collective-permute-start
  814.4 1.3 collective-permute-start.1
  815.7 1.3 collective-permute-start.10
  817.0 1.3 collective-permute-start.11
  818.3 1.3 collective-permute-start.12
  819.6 1.1 fusion.16
  820.7 136.4 %psum.14 = f32[1792]{0:T(1024)S(1)} all-reduce(f32[1792]{0:T(1024)S(1)} %get-tuple-element.4), channel_id=1, replica_groups=mesh['grp'=2,'dev'=128] {'grp','dev'}, use_global_device_ids=true, to_apply=%region_12.13 | all-reduce | flops 1792 | bytes 14336 | tf_op jit(solution)/shard_map/psum | solution.py:101
  957.1 5.5 collective-permute-start.13
  962.6 6.2 collective-permute-start.14
  968.8 3.2 collective-permute-start.2
  972.0 3.7 collective-permute-start.3
  975.7 1.5 collective-permute-start.4
  977.2 0.6 broadcast_multiply_fusion
  977.8 4.4 collective-permute-start.5
  982.2 6.2 collective-permute-start.6
  988.4 1.9 collective-permute-start.7
  990.3 3.9 collective-permute-start.8
  994.2 6.7 collective-permute-start.9
  1001.0 0.5 broadcast_multiply_fusion.2
  1001.5 0.6 copy-done.4
  1002.1 0.6 copy-done.6
  1002.8 5.3 concatenate.4
  1008.1 0.6 dynamic-slice_multiply_fusion
  (63 shorter events, 1.2 us)
Async XLA Ops:
  7.2 250.3 %copy-start = (bf16[1,768,1024]{2,1,0:T(8,128)(2,1)S(1)}, bf16[1,768,1024]{2,1,0:T(8,128)(2,1)}, u32[]{:S(2)}) copy-start(bf16[1,768,1024]{2,1,0:T(8,128)(2,1)} %param.13) | copy-start | bytes 4718596
  267.6 12.2 %copy-start.7 = (f32[128,8]{0,1:T(8,128)S(1)}, f32[128,8]{0,1:T(8,128)}, u32[]{:S(2)}) copy-start(f32[128,8]{0,1:T(8,128)} %param.11) | copy-start | bytes 12292
  267.6 12.4 %copy-start.8 = (s32[128]{0:T(128)S(1)}, s32[128]{0:T(128)}, u32[]{:S(2)}) copy-start(s32[128]{0:T(128)} %param.14) | copy-start | bytes 1540
  267.6 108.4 %all-to-all-start.1 = ((bf16[128,12,1024]{2,1,0:T(8,128)(2,1)}), bf16[128,12,1024]{2,1,0:T(8,128)(2,1)}, u32[]{:S(2)}, u32[]{:S(2)}) async-start(bf16[128,12,1024]{2,1,0:T(8,128)(2,1)} %reshape.100), calls=%async_computation.1 | async-start | bytes 8388608 | tf_op jit(solution)/shard_map/all_to_all | solution.py:67
  279.1 131.3 %all-gather.3.cloned.1.call-start = ((), (), s32[]{:S(2)}) async-start(), calls=%async_computation.4 | async-start | bytes 4227072 | tf_op jit(solution)/shard_map/all_gather | solution.py:82
  386.1 16.5 %copy-start.2 = (bf16[128,1792]{1,0:T(8,128)(2,1)S(1)}, bf16[128,1792]{1,0:T(8,128)(2,1)}, u32[]{:S(2)}) copy-start(bf16[128,1792]{1,0:T(8,128)(2,1)} %param.15) | copy-start | bytes 1376260
  391.9 25.2 %copy-start.3 = (f32[1792]{0:T(1024)S(1)}, f32[1792]{0:T(1024)}, u32[]{:S(2)}) copy-start(f32[1792]{0:T(1024)} %param.16) | copy-start | bytes 21508
  391.9 25.0 %all-to-all-start.2 = ((bf16[128,2,512]{2,1,0:T(2,128)(2,1)}), bf16[128,2,512]{2,1,0:T(2,128)(2,1)S(1)}, u32[]{:S(2)}, u32[]{:S(2)}) async-start(bf16[128,2,512]{2,1,0:T(2,128)(2,1)} %reshape.157), calls=%async_computation.2 | async-start | bytes 524288 | tf_op jit(solution)/shard_map/all_to_all | solution.py:79
  402.5 57.0 %all-reduce.5.cloned.1.call-start = ((), (), s32[]{:S(2)}) async-start(), calls=%async_computation.3 | async-start | bytes 7340032 | tf_op jit(solution)/shard_map/psum | solution.py:105
  419.9 3.1 copy-start.9
  459.5 549.2 %copy-start.1 = (bf16[1,768,1024]{2,1,0:T(8,128)(2,1)S(1)}, bf16[1,768,1024]{2,1,0:T(8,128)(2,1)}, u32[]{:S(2)}) copy-start(bf16[1,768,1024]{2,1,0:T(8,128)(2,1)} %param.13) | copy-start | bytes 4718596
  811.8 6.5 collective-permute-start.15
  813.1 144.0 %collective-permute-start = (f32[16,1024]{1,0:T(8,128)S(1)}, f32[16,1024]{1,0:T(8,128)S(1)}, u32[]{:S(2)}, u32[]{:S(2)}) collective-permute-start(f32[16,1024]{1,0:T(8,128)S(1)} %fusion), channel_id=1, source_target_pairs={{0,1},{1,2},{2,3},{3,4},{4,5},{5,6},{6,7},{7,8},{8,9},{9,10},{10,1... | collective-permute-start | bytes 196616
  814.4 148.2 %collective-permute-start.1 = (f32[16,1024]{1,0:T(8,128)S(1)}, f32[16,1024]{1,0:T(8,128)S(1)}, u32[]{:S(2)}, u32[]{:S(2)}) collective-permute-start(f32[16,1024]{1,0:T(8,128)S(1)} %fusion), channel_id=1, source_target_pairs={{0,2},{1,3},{2,4},{3,5},{4,6},{5,7},{6,8},{7,9},{8,10},{9,11},{10,... | collective-permute-start | bytes 196616
  815.7 153.1 %collective-permute-start.10 = (f32[16,1024]{1,0:T(8,128)S(1)}, f32[16,1024]{1,0:T(8,128)S(1)}, u32[]{:S(2)}, u32[]{:S(2)}) collective-permute-start(f32[16,1024]{1,0:T(8,128)S(1)} %fusion), channel_id=1, source_target_pairs={{0,11},{1,12},{2,13},{3,14},{4,15},{5,16},{6,17},{7,18},{8,19},{9,... | collective-permute-start | bytes 196616
  817.0 155.0 %collective-permute-start.11 = (f32[16,1024]{1,0:T(8,128)S(1)}, f32[16,1024]{1,0:T(8,128)S(1)}, u32[]{:S(2)}, u32[]{:S(2)}) collective-permute-start(f32[16,1024]{1,0:T(8,128)S(1)} %fusion), channel_id=1, source_target_pairs={{0,12},{1,13},{2,14},{3,15},{4,16},{5,17},{6,18},{7,19},{8,20},{9,... | collective-permute-start | bytes 196616
  818.3 157.4 %collective-permute-start.12 = (f32[16,1024]{1,0:T(8,128)S(1)}, f32[16,1024]{1,0:T(8,128)S(1)}, u32[]{:S(2)}, u32[]{:S(2)}) collective-permute-start(f32[16,1024]{1,0:T(8,128)S(1)} %fusion), channel_id=1, source_target_pairs={{0,13},{1,14},{2,15},{3,16},{4,17},{5,18},{6,19},{7,20},{8,21},{9,... | collective-permute-start | bytes 196616
  957.1 20.7 %collective-permute-start.13 = (f32[16,1024]{1,0:T(8,128)S(1)}, f32[16,1024]{1,0:T(8,128)S(1)}, u32[]{:S(2)}, u32[]{:S(2)}) collective-permute-start(f32[16,1024]{1,0:T(8,128)S(1)} %fusion), channel_id=1, source_target_pairs={{0,14},{1,15},{2,16},{3,17},{4,18},{5,19},{6,20},{7,21},{8,22},{9,... | collective-permute-start | bytes 196616
  962.6 19.6 %collective-permute-start.14 = (f32[16,1024]{1,0:T(8,128)S(1)}, f32[16,1024]{1,0:T(8,128)S(1)}, u32[]{:S(2)}, u32[]{:S(2)}) collective-permute-start(f32[16,1024]{1,0:T(8,128)S(1)} %fusion), channel_id=1, source_target_pairs={{0,15},{1,16},{2,17},{3,18},{4,19},{5,20},{6,21},{7,22},{8,23},{9,... | collective-permute-start | bytes 196616
  968.8 19.6 %collective-permute-start.2 = (f32[16,1024]{1,0:T(8,128)S(1)}, f32[16,1024]{1,0:T(8,128)S(1)}, u32[]{:S(2)}, u32[]{:S(2)}) collective-permute-start(f32[16,1024]{1,0:T(8,128)S(1)} %fusion), channel_id=1, source_target_pairs={{0,3},{1,4},{2,5},{3,6},{4,7},{5,8},{6,9},{7,10},{8,11},{9,12},{10... | collective-permute-start | bytes 196616
  972.0 18.3 %collective-permute-start.3 = (f32[16,1024]{1,0:T(8,128)S(1)}, f32[16,1024]{1,0:T(8,128)S(1)}, u32[]{:S(2)}, u32[]{:S(2)}) collective-permute-start(f32[16,1024]{1,0:T(8,128)S(1)} %fusion), channel_id=1, source_target_pairs={{0,4},{1,5},{2,6},{3,7},{4,8},{5,9},{6,10},{7,11},{8,12},{9,13},{1... | collective-permute-start | bytes 196616
  975.7 18.5 %collective-permute-start.4 = (f32[16,1024]{1,0:T(8,128)S(1)}, f32[16,1024]{1,0:T(8,128)S(1)}, u32[]{:S(2)}, u32[]{:S(2)}) collective-permute-start(f32[16,1024]{1,0:T(8,128)S(1)} %fusion), channel_id=1, source_target_pairs={{0,5},{1,6},{2,7},{3,8},{4,9},{5,10},{6,11},{7,12},{8,13},{9,14},{... | collective-permute-start | bytes 196616
  977.8 23.7 %collective-permute-start.5 = (f32[16,1024]{1,0:T(8,128)S(1)}, f32[16,1024]{1,0:T(8,128)S(1)}, u32[]{:S(2)}, u32[]{:S(2)}) collective-permute-start(f32[16,1024]{1,0:T(8,128)S(1)} %fusion), channel_id=1, source_target_pairs={{0,6},{1,7},{2,8},{3,9},{4,10},{5,11},{6,12},{7,13},{8,14},{9,15},... | collective-permute-start | bytes 196616
  982.2 19.3 %collective-permute-start.6 = (f32[16,1024]{1,0:T(8,128)S(1)}, f32[16,1024]{1,0:T(8,128)S(1)}, u32[]{:S(2)}, u32[]{:S(2)}) collective-permute-start(f32[16,1024]{1,0:T(8,128)S(1)} %fusion), channel_id=1, source_target_pairs={{0,7},{1,8},{2,9},{3,10},{4,11},{5,12},{6,13},{7,14},{8,15},{9,16}... | collective-permute-start | bytes 196616
  988.4 13.1 %collective-permute-start.7 = (f32[16,1024]{1,0:T(8,128)S(1)}, f32[16,1024]{1,0:T(8,128)S(1)}, u32[]{:S(2)}, u32[]{:S(2)}) collective-permute-start(f32[16,1024]{1,0:T(8,128)S(1)} %fusion), channel_id=1, source_target_pairs={{0,8},{1,9},{2,10},{3,11},{4,12},{5,13},{6,14},{7,15},{8,16},{9,17... | collective-permute-start | bytes 196616
  990.3 11.2 %collective-permute-start.8 = (f32[16,1024]{1,0:T(8,128)S(1)}, f32[16,1024]{1,0:T(8,128)S(1)}, u32[]{:S(2)}, u32[]{:S(2)}) collective-permute-start(f32[16,1024]{1,0:T(8,128)S(1)} %fusion), channel_id=1, source_target_pairs={{0,9},{1,10},{2,11},{3,12},{4,13},{5,14},{6,15},{7,16},{8,17},{9,1... | collective-permute-start | bytes 196616
  994.2 8.5 collective-permute-start.9
  1001.5 0.6 copy-start.4
  1001.5 0.6 copy-start.5
  1002.1 0.6 copy-start.6
Sparse Core Ops, SparseCore 0:
  283.6 126.7 all-gather.2
  423.1 36.3 all-reduce.4
where the time goes:
time: 1020 us
  blocking collectives  682 us (67%)
  waiting for transfers between devices  135 us (13%)
  starting transfers between devices  73.1 us (7%)
  local copies, waits for them, and re-layouts  68.7 us (7%)
  matrix products  29.9 us (3%)
  between operations  15.2 us (1%)
  other arithmetic  12 us (1%)
    unnamed x1, blocking collectives  346 us
    all_to_all x1, blocking collectives, body(): lax.all_to_all(outgoing, 'dev', split_axis=0, concat_axis=0, tiled=True)  199 us
    psum x1, blocking collectives, body(): lax.psum(jnp.sum(normed_grad * unit_rows, axis=0), ('grp', 'dev'))  136 us
    all_to_all x1, waiting for transfers between devices, body(): lax.all_to_all(produced, 'dev', split_axis=0, concat_axis=0, tiled=True)  94.5 us
    unnamed x16, starting transfers between devices  50.9 us
    psum x1, waiting for transfers between devices, body(): lax.psum(whole_term.astype(jnp.bfloat16), 'grp').astype(jnp.float32)  31.7 us
  transfers between devices with their start and end apart: 20, of which 3 were waited for; matrix products, arithmetic and copies ran while one was open for 3% of the time, Pallas kernels for 0%

commit v1 on v0

--- a/solution.py
+++ b/solution.py
@@ -3,9 +3,13 @@
 import jax
 import jax.numpy as jnp
 from jax import lax
+from jax.sharding import Mesh
 from jax.sharding import PartitionSpec as P
 
 epsilon = 1e-06
+DEV = ("x", "z", "y")
+DEV_SHAPE = (4, 8, 4)
+SWAP = ((0, 1), (1, 0))
 
 
 def expert_rows(inputs, gate_up, down_proj):
@@ -43,7 +47,7 @@
     tok_rows = teacher_input.shape[0]
     top_count = expert_routes.shape[1]
     width_in = teacher_input.shape[1]
-    owner_count = lax.axis_size("dev")
+    owner_count = lax.axis_size(DEV)
     capacity = 3 * tok_rows * top_count // (2 * owner_count)
     pair_count = tok_rows * top_count
     flat_routes = expert_routes.reshape(-1)
@@ -59,12 +63,12 @@
     outgoing = padded[source_rows].reshape(owner_count, capacity, width_in)
     gate_up = expert_gate_up[0]
     down_proj = expert_down[0]
-    arrived = lax.all_to_all(outgoing, "dev", split_axis=0, concat_axis=0, tiled=True)
+    arrived = lax.all_to_all(outgoing, DEV, split_axis=0, concat_axis=0, tiled=True)
     senders = arrived.shape[0]
     slot_count = arrived.shape[1]
     produced = expert_rows(arrived.reshape(senders * slot_count, width_in), gate_up, down_proj)
     produced = produced.reshape(senders, slot_count, down_proj.shape[1])
-    returned = lax.all_to_all(produced, "dev", split_axis=0, concat_axis=0, tiled=True)
+    returned = lax.all_to_all(produced, DEV, split_axis=0, concat_axis=0, tiled=True)
     picked = returned.reshape(owner_count * capacity, -1)[slot_place].reshape(
         tok_rows, top_count, -1
     )
@@ -77,17 +81,46 @@
     )
     relay_rows = teacher_target[inverse].reshape(owner_count, per_owner, -1)
     student_target = lax.all_to_all(
-        relay_rows, "dev", split_axis=0, concat_axis=0, tiled=True
+        relay_rows, DEV, split_axis=0, concat_axis=0, tiled=True
     ).reshape(tok_rows, -1)
-    full_weight = lax.all_gather(align_weight, "dev", axis=0, tiled=True)
+    full_weight = lax.all_gather(align_weight, DEV, axis=0, tiled=True)
     inputs_f = student_input.astype(jnp.float32)
     scale_rows = row_scale(inputs_f)
     unit_rows = inputs_f * scale_rows
     normed = (unit_rows * student_gain).astype(jnp.bfloat16)
     student_out = jnp.dot(normed, full_weight, preferred_element_type=jnp.float32)
+    size_x, size_z, size_y = (lax.axis_size(name) for name in DEV)
+    shard_rows = align_weight.shape[0]
+    normed_z = (
+        normed.reshape(tok_rows, size_x, size_z, size_y * shard_rows)
+        .transpose(0, 2, 1, 3)
+        .reshape(tok_rows, -1)
+    )
+    normed_pair = jnp.concatenate([normed_z, lax.ppermute(normed_z, "grp", SWAP)], axis=0)
     distance = student_out - student_target.astype(jnp.float32)
     token_loss = jnp.mean(distance * distance, axis=-1)
     distance_bf = distance.astype(jnp.bfloat16)
+    core = lax.axis_index("grp")
+    half = distance_bf.shape[1] // 2
+    low, high = distance_bf[:, :half], distance_bf[:, half:]
+    kept = jnp.where(core == 0, low, high)
+    given = jnp.where(core == 0, high, low)
+    distance_pair = jnp.concatenate([kept, lax.ppermute(given, "grp", SWAP)], axis=0)
+    term = lax.dot_general(
+        normed_pair, distance_pair, (((0,), (0,)), ((), ())), preferred_element_type=jnp.float32
+    ).astype(jnp.bfloat16)
+    term = lax.psum_scatter(term, "z", scatter_dimension=0, tiled=True)
+    term = term.reshape(size_x * size_y, shard_rows, half)
+    term = lax.all_to_all(term, ("x", "y"), split_axis=0, concat_axis=0, tiled=True)
+    tokens_all = tok_rows * lax.axis_size("grp") * owner_count
+    grad_factor = 1.0 / math.sqrt(tokens_all)
+    shard_half = jnp.sum(term.astype(jnp.float32), axis=0) * grad_factor
+    other_half = lax.ppermute(shard_half, "grp", SWAP)
+    align_grad = jnp.where(
+        core == 0,
+        jnp.concatenate([shard_half, other_half], axis=1),
+        jnp.concatenate([other_half, shard_half], axis=1),
+    )
     normed_grad = lax.dot_general(
         distance_bf, full_weight, (((1,), (1,)), ((), ())), preferred_element_type=jnp.float32
     )
@@ -96,34 +129,31 @@
         scale_rows
         * (gain_inner - unit_rows * jnp.mean(gain_inner * unit_rows, axis=-1, keepdims=True))
     ).astype(jnp.bfloat16)
-    tokens_all = tok_rows * lax.axis_size("grp") * owner_count
-    grad_factor = 1.0 / math.sqrt(tokens_all)
-    gain_grad = lax.psum(jnp.sum(normed_grad * unit_rows, axis=0), ("grp", "dev")) * grad_factor
-    whole_term = lax.dot_general(
-        normed, distance_bf, (((0,), (0,)), ((), ())), preferred_element_type=jnp.float32
-    )
-    summed = lax.psum(whole_term.astype(jnp.bfloat16), "grp").astype(jnp.float32)
-    shard_part = lax.psum_scatter(summed, "dev", scatter_dimension=0, tiled=True)
-    align_grad = shard_part * grad_factor
+    gain_part = jnp.sum(normed_grad * unit_rows, axis=0)
+    gain_part = jnp.sum(lax.all_gather(gain_part, ("grp", "z"), axis=0), axis=0)
+    gain_part = jnp.sum(lax.all_gather(gain_part, ("x", "y"), axis=0), axis=0)
+    gain_grad = gain_part * grad_factor
     return (token_loss, input_grad, gain_grad, align_grad)
 
 
 def solution(mesh):
+    grid = Mesh(mesh.devices.reshape((mesh.devices.shape[0],) + DEV_SHAPE), ("grp",) + DEV)
+    tokens = ("grp",) + DEV
     placed = (
-        P(("grp", "dev"), None),
-        P(("grp", "dev"), None),
-        P(("grp", "dev"), None),
-        P("dev", None, None),
-        P("dev", None, None),
-        P(("grp", "dev")),
-        P(("grp", "dev"), None),
+        P(tokens, None),
+        P(tokens, None),
+        P(tokens, None),
+        P(DEV, None, None),
+        P(DEV, None, None),
+        P(tokens),
+        P(tokens, None),
         P(),
-        P("dev", None),
+        P(DEV, None),
     )
     return jax.shard_map(
         body,
-        mesh=mesh,
+        mesh=grid,
         in_specs=placed,
-        out_specs=(P(("grp", "dev")), P(("grp", "dev"), None), P(), P("dev", None)),
+        out_specs=(P(tokens), P(tokens, None), P(), P(DEV, None)),
         check_vma=False,
     )

time: 1020 us -> 507 us (0.50)
  blocking collectives: 682 us -> 242 us
  starting transfers between devices: 73.1 us -> 38.4 us
  waiting for transfers between devices: 135 us -> 105 us
    unnamed x1 -> x0, blocking collectives: 346 us -> none
    psum x1 -> x0, blocking collectives: 136 us -> none  [body(): lax.psum(jnp.sum(normed_grad * unit_rows, axis=0), ('grp', 'dev'))]
    unnamed x16 -> x0, starting transfers between devices: 50.9 us -> none
    all_gather x0 -> x2, blocking collectives: none -> 42.6 us  [the longest x1 26.5 us: body(): gain_part = jnp.sum(lax.all_gather(gain_part, ('grp', 'z'), axis=0), axis=0)]
    psum x1 -> x0, waiting for transfers between devices: 31.7 us -> none  [body(): lax.psum(whole_term.astype(jnp.bfloat16), 'grp').astype(jnp.float32)]
    ppermute x0 -> x3, starting transfers between devices: none -> 11.5 us  [the longest x1 6.01 us: body(): other_half = lax.ppermute(shard_half, 'grp', SWAP)]
    all_to_all x2 -> x3, waiting for transfers between devices: 94.5 us -> 103 us  [the longest x1 94.3 us: body(): lax.all_to_all(produced, DEV, split_axis=0, concat_axis=0, tiled=True)]
    all_to_all x2 -> x3, starting transfers between devices: 22.1 us -> 26.9 us  [the longest x1 11.5 us: body(): lax.all_to_all(produced, DEV, split_axis=0, concat_axis=0, tiled=True)]
  transfers between devices with their start and end apart: 20 -> 8, of which waited for: 3 -> 5; matrix products, arithmetic and copies ran while one was open for 3% -> 8% of each run, Pallas kernels for 0% -> 0%
where the time goes in v1:
time: 507 us; the launch traced here: 505 us
  blocking collectives  242 us (48%)
  waiting for transfers between devices  105 us (21%)
  local copies, waits for them, and re-layouts  68.7 us (14%)
  starting transfers between devices  38.4 us (8%)
  matrix products  29.8 us (6%)
  between operations  14.4 us (3%)
  other arithmetic  6.34 us (1%)
    all_to_all x1, blocking collectives, body(): lax.all_to_all(outgoing, DEV, split_axis=0, concat_axis=0, tiled=True)  199 us
    all_to_all x1, waiting for transfers between devices, body(): lax.all_to_all(produced, DEV, split_axis=0, concat_axis=0, tiled=True)  94.3 us
    all_gather x1, blocking collectives, body(): gain_part = jnp.sum(lax.all_gather(gain_part, ('grp', 'z'), axis=0), axis=0)  26.5 us
    all_gather x1, blocking collectives, body(): gain_part = jnp.sum(lax.all_gather(gain_part, ('x', 'y'), axis=0), axis=0)  16.2 us
    dot_general x1, matrix products, expert_rows(): hidden_both = jnp.dot(inputs, gate_up, preferred_element_type=jnp.float32)  14.1 us
    all_to_all x1, starting transfers between devices, body(): lax.all_to_all(produced, DEV, split_axis=0, concat_axis=0, tiled=True)  11.5 us
    reshape x1, local copies, waits for them, and re-layouts, body(): arrived.reshape(senders * slot_count, width_in)  10.7 us
    reshape x1, local copies, waits for them, and re-layouts, body(): outgoing = padded[source_rows].reshape(owner_count, capacity, width_in)  10.6 us
  transfers between devices with their start and end apart: 8, of which 5 were waited for; matrix products, arithmetic and copies ran while one was open for 8% of the time, Pallas kernels for 0%

profile of v1, /device:TPU:1, one launch (start us, length us, event | category | flops | bytes accessed | tf_op | source)
XLA Modules:
  0.0 505.0 jit_solution(12139815675040804434)
XLA Ops:
  7.2 0.9 copy.21
  8.1 0.1 eq.47
  8.2 0.1 eq.43
  8.3 0.7 broadcast_multiply_fusion.2
  9.0 0.1 copy.23
  9.1 0.2 fusion.25
  9.4 0.1 copy.24
  9.5 0.1 copy.20
  9.6 0.1 mul.107
  9.7 0.4 fusion.22
  10.1 4.3 scatter_custom_fusion
  14.4 1.1 concatenate.15
  15.5 7.1 %gather_fusion = bf16[1536,2048]{1,0:T(8,128)(2,1)} fusion(bf16[129,2048]{1,0:T(8,128)(2,1)S(1)} %concatenate.15, s32[2048]{0:T(1024)S(1)} %pad_clamp_fusion), kind=kCustom, calls=%fused_computation | custom fusion | bytes 12589056 | tf_op jit(solution)/shard_map/gather | solution.py:63
  22.6 10.6 %reshape.107 = bf16[128,12,2048]{2,1,0:T(8,128)(2,1)} reshape(bf16[1536,2048]{1,0:T(8,128)(2,1)} %gather_fusion) | data formatting | bytes 12582912 | tf_op jit(solution)/shard_map/reshape | solution.py:63
  33.2 199.5 %all_to_all.20 = bf16[128,12,2048]{2,1,0:T(8,128)(2,1)} all-to-all(bf16[128,12,2048]{2,1,0:T(8,128)(2,1)} %reshape.107), channel_id=1, replica_groups=mesh['grp'=2,'x'=4,'z'=8,'y'=4] {'x','z','y'}, dimensions={0} | all-to-all | bytes 12582912 | tf_op jit(solution)/shard_map/all_to_all | solution.py:66
  232.7 10.7 %reshape.108 = bf16[1536,2048]{1,0:T(8,128)(2,1)} reshape(bf16[128,12,2048]{2,1,0:T(8,128)(2,1)} %all_to_all.20) | data formatting | bytes 12582912 | tf_op jit(solution)/shard_map/reshape | solution.py:69
  243.4 14.1 %fusion = f32[1536,1536]{1,0:T(8,128)S(1)} fusion(bf16[1536,2048]{1,0:T(8,128)(2,1)} %reshape.108, bf16[1,2048,1536]{2,1,0:T(8,128)(2,1)} %param.12), kind=kOutput, calls=%fused_computation.5 | convolution fusion | flops 9663676416 | bytes 22020096 | tf_op jit(solution)/shard_map/dot_general | solution.py:16
  257.5 4.0 convolution_convert_fusion
  261.5 6.1 %reshape.109 = bf16[128,12,1024]{2,1,0:T(8,128)(2,1)} reshape(bf16[1536,1024]{1,0:T(8,128)(2,1)} %convolution_convert_fusion) | data formatting | bytes 6291456 | tf_op jit(solution)/shard_map/reshape | solution.py:70
  267.6 11.5 %all-to-all-start.1 = ((bf16[128,12,1024]{2,1,0:T(8,128)(2,1)}), bf16[128,12,1024]{2,1,0:T(8,128)(2,1)}, u32[]{:S(2)}, u32[]{:S(2)}) async-start(bf16[128,12,1024]{2,1,0:T(8,128)(2,1)} %reshape.109), calls=%async_computation.1 | async-start | bytes 8388608 | tf_op jit(solution)/shard_map/all_to_all | solution.py:71
  279.1 0.7 all-gather.7.cloned.1.call-update
  279.8 0.1 copy.29
  280.0 0.1 fusion.31
  280.1 0.2 reduce_window_sum.28
  280.3 0.2 select_reduce_fusion
  280.5 1.0 scatter_custom_fusion.1
  281.5 0.2 fusion.17
  281.7 94.3 %all-to-all-done.1 = bf16[128,12,1024]{2,1,0:T(8,128)(2,1)} async-done(((bf16[128,12,1024]{2,1,0:T(8,128)(2,1)}), bf16[128,12,1024]{2,1,0:T(8,128)(2,1)}, u32[]{:S(2)}, u32[]{:S(2)}) %all-to-all-start.1) | async-done | bytes 3145760 | tf_op jit(solution)/shard_map/all_to_all | solution.py:71
  376.0 6.2 %reshape.110 = bf16[1536,1024]{1,0:T(8,128)(2,1)} reshape(bf16[128,12,1024]{2,1,0:T(8,128)(2,1)} %all-to-all-done.1) | data formatting | bytes 6291456 | tf_op jit(solution)/shard_map/reshape | solution.py:72
  382.2 8.3 %gather_fusion.1 = bf16[1024,1024]{1,0:T(8,128)(2,1)} fusion(bf16[1536,1024]{1,0:T(8,128)(2,1)} %reshape.110, s32[1024]{0:T(1024)S(1)} %broadcast_clamp_fusion), kind=kCustom, calls=%fused_computation.1 | custom fusion | bytes 4198400 | tf_op jit(solution)/shard_map/gather | solution.py:72
  390.5 2.3 fusion.4
  392.8 0.2 fusion.23
  393.0 0.2 fusion.24
  393.1 0.9 gather_fusion.2
  394.0 0.5 broadcast.145
  394.5 0.8 reduce.2
  395.3 0.9 reshape.176
  396.2 10.6 %all-to-all-start.2 = ((bf16[128,2,512]{2,1,0:T(2,128)(2,1)}), bf16[128,2,512]{2,1,0:T(2,128)(2,1)S(1)}, u32[]{:S(2)}, u32[]{:S(2)}) async-start(bf16[128,2,512]{2,1,0:T(2,128)(2,1)} %reshape.176), calls=%async_computation.2 | async-start | bytes 524288 | tf_op jit(solution)/shard_map/all_to_all | solution.py:83
  406.9 0.2 fusion.11
  407.1 0.3 copy.27
  407.3 0.8 copy.28
  408.1 1.9 collective-permute-start
  410.0 6.4 %reshape.163 = bf16[1792,1024]{1,0:T(8,128)(2,1)} reshape(bf16[128,14,1024]{2,1,0:T(8,128)(2,1)} %all-gather.7.cloned.1.call-done) | data formatting | bytes 7340032
  416.5 2.2 all-to-all-done.2
  418.6 0.2 reshape.177
  418.9 2.8 fusion.41
  421.8 3.6 collective-permute-start.1
  425.4 1.0 collective-permute-done.1
  426.3 3.0 convolution_convert_fusion.1
  429.4 3.5 fusion.16
  432.9 26.5 %all-gather.3 = f32[16,1,1792]{2,1,0:T(1,128)S(1)} all-gather(f32[1,1,1792]{2,1,0:T(1,128)S(1)} %reshape.164), channel_id=2, replica_groups=mesh['grp'=2,'x'=4,'z'=8,'y'=4] {'grp','z'}, dimensions={0}, use_global_device_ids=true | all-gather | bytes 121856 | tf_op jit(solution)/shard_map/all_gather | solution.py:133
  459.4 0.1 reduce_sum.100
  459.5 16.2 %all-gather.4 = f32[16,1,1792]{2,1,0:T(1,128)S(1)} all-gather(f32[1,1,1792]{2,1,0:T(1,128)S(1)} %reshape.166), channel_id=3, replica_groups=mesh['grp'=2,'x'=4,'z'=8,'y'=4] {'x','y'}, dimensions={0}, use_global_device_ids=true | all-gather | bytes 121856 | tf_op jit(solution)/shard_map/all_gather | solution.py:134
  475.7 0.1 reduce_sum.101
  475.8 1.1 fusion.15
  476.8 1.7 reshape.115
  478.5 4.8 all-to-all-start.3
  483.3 0.6 broadcast_multiply_fusion.1
  483.9 6.7 %all-to-all-done.3 = bf16[16,14,512]{2,1,0:T(8,128)(2,1)S(1)} async-done(((bf16[16,14,512]{2,1,0:T(8,128)(2,1)}), bf16[16,14,512]{2,1,0:T(8,128)(2,1)S(1)}, u32[]{:S(2)}, u32[]{:S(2)}) %all-to-all-start.3) | async-done | bytes 229408 | tf_op jit(solution)/shard_map/all_to_all | solution.py:114
  490.6 0.1 convert_reduce_fusion
  490.7 6.0 %collective-permute-start.2 = (f32[14,512]{1,0:T(8,128)S(1)}, f32[14,512]{1,0:T(8,128)S(1)}, u32[]{:S(2)}, u32[]{:S(2)}) collective-permute-start(f32[14,512]{1,0:T(8,128)S(1)} %broadcast_multiply_fusion), channel_id=1, source_target_pairs={{0,128},{128,0},{1,129},{129,1},{2,130},{130,2},{3,131},{131,3},{4... | collective-permute-start | bytes 86024 | tf_op jit(solution)/shard_map/ppermute | solution.py:118
  496.7 0.5 broadcast_multiply_fusion.3
  497.2 0.3 collective-permute-done.2
  497.6 0.6 maximum_select_fusion
  (36 shorter events, 0.3 us)
Async XLA Ops:
  7.2 250.3 %copy-start = (bf16[1,768,1024]{2,1,0:T(8,128)(2,1)S(1)}, bf16[1,768,1024]{2,1,0:T(8,128)(2,1)}, u32[]{:S(2)}) copy-start(bf16[1,768,1024]{2,1,0:T(8,128)(2,1)} %param.13) | copy-start | bytes 4718596
  267.6 12.3 %copy-start.3 = (f32[128,8]{0,1:T(8,128)S(1)}, f32[128,8]{0,1:T(8,128)}, u32[]{:S(2)}) copy-start(f32[128,8]{0,1:T(8,128)} %param.11) | copy-start | bytes 12292
  267.6 12.4 %copy-start.4 = (s32[128]{0:T(128)S(1)}, s32[128]{0:T(128)}, u32[]{:S(2)}) copy-start(s32[128]{0:T(128)} %param.14) | copy-start | bytes 1540
  267.6 13.9 %copy-start.1 = (bf16[128,1792]{1,0:T(8,128)(2,1)S(1)}, bf16[128,1792]{1,0:T(8,128)(2,1)}, u32[]{:S(2)}) copy-start(bf16[128,1792]{1,0:T(8,128)(2,1)} %param.15) | copy-start | bytes 1376260
  267.6 108.4 %all-to-all-start.1 = ((bf16[128,12,1024]{2,1,0:T(8,128)(2,1)}), bf16[128,12,1024]{2,1,0:T(8,128)(2,1)}, u32[]{:S(2)}, u32[]{:S(2)}) async-start(bf16[128,12,1024]{2,1,0:T(8,128)(2,1)} %reshape.109), calls=%async_computation.1 | async-start | bytes 8388608 | tf_op jit(solution)/shard_map/all_to_all | solution.py:71
  279.1 130.9 %all-gather.7.cloned.1.call-start = ((), (), s32[]{:S(2)}) async-start(), calls=%async_computation.6 | async-start | bytes 4227072 | tf_op jit(solution)/shard_map/all_gather | solution.py:86
  390.5 16.4 %copy-start.2 = (f32[1792]{0:T(1024)S(1)}, f32[1792]{0:T(1024)}, u32[]{:S(2)}) copy-start(f32[1792]{0:T(1024)} %param.16) | copy-start | bytes 21508
  396.2 22.4 %all-to-all-start.2 = ((bf16[128,2,512]{2,1,0:T(2,128)(2,1)}), bf16[128,2,512]{2,1,0:T(2,128)(2,1)S(1)}, u32[]{:S(2)}, u32[]{:S(2)}) async-start(bf16[128,2,512]{2,1,0:T(2,128)(2,1)} %reshape.176), calls=%async_computation.2 | async-start | bytes 524288 | tf_op jit(solution)/shard_map/all_to_all | solution.py:83
  406.8 70.0 %reduce-scatter.2.cloned.1.call-start = ((), (), s32[]{:S(2)}) async-start(), calls=%async_computation.5 | async-start | bytes 2064384 | tf_op jit(solution)/shard_map/reduce_scatter | solution.py:112
  408.1 17.2 %collective-permute-start = (bf16[128,1792]{0,1:T(8,128)(2,1)}, bf16[128,1792]{0,1:T(8,128)(2,1)}, u32[]{:S(2)}, u32[]{:S(2)}) collective-permute-start(bf16[128,1792]{0,1:T(8,128)(2,1)} %bitcast.15), channel_id=1, source_target_pairs={{0,128},{128,0},{1,129},{129,1},{2,130},{130,2},{3,131},{131,3},{4... | collective-permute-start | bytes 1376264 | tf_op jit(solution)/shard_map/ppermute | solution.py:99
  421.8 4.6 collective-permute-start.1
  478.5 12.1 %all-to-all-start.3 = ((bf16[16,14,512]{2,1,0:T(8,128)(2,1)}), bf16[16,14,512]{2,1,0:T(8,128)(2,1)S(1)}, u32[]{:S(2)}, u32[]{:S(2)}) async-start(bf16[16,14,512]{2,1,0:T(8,128)(2,1)} %reshape.115), calls=%async_computation.4 | async-start | bytes 524288 | tf_op jit(solution)/shard_map/all_to_all | solution.py:114
  490.7 6.9 %collective-permute-start.2 = (f32[14,512]{1,0:T(8,128)S(1)}, f32[14,512]{1,0:T(8,128)S(1)}, u32[]{:S(2)}, u32[]{:S(2)}) collective-permute-start(f32[14,512]{1,0:T(8,128)S(1)} %broadcast_multiply_fusion), channel_id=1, source_target_pairs={{0,128},{128,0},{1,129},{129,1},{2,130},{130,2},{3,131},{131,3},{4... | collective-permute-start | bytes 86024 | tf_op jit(solution)/shard_map/ppermute | solution.py:118
Sparse Core Ops, SparseCore 0:
  283.6 124.3 all-gather.6
  429.5 32.6 reduce-scatter.1

commit v2 on v1

--- a/solution.py
+++ b/solution.py
@@ -10,6 +10,11 @@
 DEV = ("x", "z", "y")
 DEV_SHAPE = (4, 8, 4)
 SWAP = ((0, 1), (1, 0))
+GROUPS = ((0, 1), (-1, 2, -2, 3), (-3, 4))
+
+
+def shifts(count, by):
+    return [(i, (i + by) % count) for i in range(count)]
 
 
 def expert_rows(inputs, gate_up, down_proj):
@@ -46,33 +51,71 @@
 ):
     tok_rows = teacher_input.shape[0]
     top_count = expert_routes.shape[1]
-    width_in = teacher_input.shape[1]
     owner_count = lax.axis_size(DEV)
-    capacity = 3 * tok_rows * top_count // (2 * owner_count)
-    pair_count = tok_rows * top_count
-    flat_routes = expert_routes.reshape(-1)
-    route_slot = rank_within(flat_routes, owner_count)
-    slot_place = flat_routes * capacity + route_slot
-    slot_table = (
-        jnp.full((owner_count * capacity,), pair_count, jnp.int32)
-        .at[slot_place]
-        .set(jnp.arange(pair_count, dtype=jnp.int32))
-    )
-    padded = jnp.concatenate([teacher_input, jnp.zeros((1, width_in), teacher_input.dtype)], axis=0)
-    source_rows = jnp.where(slot_table < pair_count, slot_table // top_count, tok_rows)
-    outgoing = padded[source_rows].reshape(owner_count, capacity, width_in)
     gate_up = expert_gate_up[0]
     down_proj = expert_down[0]
-    arrived = lax.all_to_all(outgoing, DEV, split_axis=0, concat_axis=0, tiled=True)
-    senders = arrived.shape[0]
-    slot_count = arrived.shape[1]
-    produced = expert_rows(arrived.reshape(senders * slot_count, width_in), gate_up, down_proj)
-    produced = produced.reshape(senders, slot_count, down_proj.shape[1])
-    returned = lax.all_to_all(produced, DEV, split_axis=0, concat_axis=0, tiled=True)
-    picked = returned.reshape(owner_count * capacity, -1)[slot_place].reshape(
-        tok_rows, top_count, -1
-    )
-    teacher_out = jnp.einsum("tk,tkd->td", route_gates, picked.astype(jnp.float32))
+    size_x, size_z, size_y = (lax.axis_size(name) for name in DEV)
+    plane = lax.axis_index("z")
+    capacity = 3 * tok_rows * top_count // (2 * owner_count)
+
+    held = {0: teacher_input}
+    for step in range(1, size_z // 2 + 1):
+        held[step] = lax.ppermute(held[step - 1], "z", shifts(size_z, -1))
+        if step > 1:
+            held[1 - step] = lax.ppermute(held[2 - step], "z", shifts(size_z, 1))
+
+    info = jnp.concatenate([expert_routes.T.astype(jnp.float32), route_gates.T], axis=0)
+    info = lax.all_gather(info, "z", axis=0)
+    info = lax.dynamic_slice_in_dim(jnp.concatenate([info, info], axis=0), plane, size_z, axis=0)
+    expert_ids = (
+        jnp.arange(size_x)[:, None] * (size_z * size_y) + plane * size_y + jnp.arange(size_y)[None, :]
+    ).reshape(-1)
+    named = info[:, None, :top_count, :] == expert_ids.astype(jnp.float32)[None, :, None, None]
+    chosen = jnp.any(named, axis=2)
+    gate_of = jnp.sum(jnp.where(named, info[:, None, top_count:, :], 0.0), axis=2)
+    before = (jnp.arange(tok_rows)[:, None] < jnp.arange(tok_rows)[None, :]).astype(jnp.bfloat16)
+    rank = jnp.dot(chosen.astype(jnp.bfloat16), before, preferred_element_type=jnp.float32)
+    slot = jnp.where(chosen, rank.astype(jnp.int32), -size_z * capacity)
+    plane_experts = size_x * size_y
+    width_in = teacher_input.shape[1]
+    width_out = down_proj.shape[1]
+
+    teacher_out = jnp.zeros((tok_rows, width_out), jnp.float32)
+    for group in GROUPS:
+        count = len(group)
+        slots = count * capacity
+        places = [offset % size_z for offset in group]
+        spot = jnp.concatenate([slot[q] + n * capacity for n, q in enumerate(places)], axis=1)
+        gates = jnp.concatenate([gate_of[q] for q in places], axis=1)
+        hot = spot[:, None, :] == jnp.arange(slots)[None, :, None]
+        pick = hot.astype(jnp.bfloat16).reshape(plane_experts * slots, count * tok_rows)
+        feats = jnp.concatenate([held[offset] for offset in group], axis=0)
+        outgoing = jnp.dot(pick, feats, preferred_element_type=jnp.float32).astype(jnp.bfloat16)
+        arrived = lax.all_to_all(
+            outgoing.reshape(plane_experts, slots, width_in),
+            ("x", "y"), split_axis=0, concat_axis=0, tiled=True,
+        )
+        produced = expert_rows(arrived.reshape(-1, width_in), gate_up, down_proj)
+        returned = lax.all_to_all(
+            produced.reshape(plane_experts, slots, width_out),
+            ("x", "y"), split_axis=0, concat_axis=0, tiled=True,
+        ).reshape(-1, width_out)
+        weights = jnp.where(hot, gates[:, None, :], 0.0).reshape(pick.shape)
+        coarse = weights.astype(jnp.bfloat16)
+        fine = (weights - coarse.astype(jnp.float32)).astype(jnp.bfloat16)
+        summed = sum(
+            lax.dot_general(
+                term, returned, (((0,), (0,)), ((), ())), preferred_element_type=jnp.float32
+            )
+            for term in (coarse, fine)
+        )
+        for n, offset in enumerate(group):
+            part = summed[n * tok_rows : (n + 1) * tok_rows]
+            if offset:
+                part = lax.ppermute(
+                    part.astype(jnp.bfloat16), "z", shifts(size_z, offset)
+                ).astype(jnp.float32)
+            teacher_out = teacher_out + part
     teacher_target = (teacher_out * row_scale(teacher_out)).astype(jnp.bfloat16)
     per_owner = tok_rows // owner_count
     owner_place = student_owner * per_owner + rank_within(student_owner, owner_count)
@@ -89,7 +132,6 @@
     unit_rows = inputs_f * scale_rows
     normed = (unit_rows * student_gain).astype(jnp.bfloat16)
     student_out = jnp.dot(normed, full_weight, preferred_element_type=jnp.float32)
-    size_x, size_z, size_y = (lax.axis_size(name) for name in DEV)
     shard_rows = align_weight.shape[0]
     normed_z = (
         normed.reshape(tok_rows, size_x, size_z, size_y * shard_rows)

time: 507 us -> 364 us (0.72)
  blocking collectives: 242 us -> 70.3 us
  starting transfers between devices: 38.4 us -> 106 us
  local copies, waits for them, and re-layouts: 68.7 us -> 14.3 us
  matrix products: 29.8 us -> 45.7 us
    all_to_all x1 -> x0, blocking collectives: 199 us -> none  [body(): lax.all_to_all(outgoing, DEV, split_axis=0, concat_axis=0, tiled=True)]
    all_to_all x1 -> x6, waiting for transfers between devices: 94.3 us -> 38.5 us  [the longest x3 29.9 us: body(): lax.all_to_all(outgoing.reshape(plane_experts, slots, width_in), ('x', 'y...]
    ppermute x0 -> x14, waiting for transfers between devices: none -> 41.1 us  [the longest x7 26.7 us: body(): lax.ppermute(part.astype(jnp.bfloat16), 'z', shifts(size_z, offset))]
    reshape x4 -> x0, local copies, waits for them, and re-layouts: 33.5 us -> none  [the longest x1 10.7 us: body(): arrived.reshape(senders * slot_count, width_in)]
    ppermute x0 -> x14, starting transfers between devices: none -> 31.2 us  [the longest x7 15.9 us: body(): lax.ppermute(part.astype(jnp.bfloat16), 'z', shifts(size_z, offset))]
    all_to_all x1 -> x6, starting transfers between devices: 11.5 us -> 39.7 us  [the longest x3 21 us: body(): lax.all_to_all(produced.reshape(plane_experts, slots, width_out), ('x', '...]
    all_gather x0 -> x1, blocking collectives: none -> 23.9 us  [body(): info = lax.all_gather(info, 'z', axis=0)]
    gather x2 -> x0, local copies, waits for them, and re-layouts: 15.4 us -> none  [the longest x1 8.34 us: body(): returned.reshape(owner_count * capacity, -1)[slot_place]]
  transfers between devices with their start and end apart: 8 -> 27, of which waited for: 5 -> 18; matrix products, arithmetic and copies ran while one was open for 8% -> 16% of each run, Pallas kernels for 0% -> 0%
where the time goes in v2:
time: 364 us; the launch traced here: 363 us
  starting transfers between devices  106 us (29%)
  waiting for transfers between devices  104 us (29%)
  blocking collectives  70.3 us (19%)
  matrix products  45.7 us (13%)
  between operations  14.6 us (4%)
  local copies, waits for them, and re-layouts  14.3 us (4%)
  other arithmetic  7.61 us (2%)
    all_to_all x3, waiting for transfers between devices, body(): lax.all_to_all(outgoing.reshape(plane_experts, slots, width_in), ('x', 'y...  29.9 us
    all_gather x1, blocking collectives, body(): gain_part = jnp.sum(lax.all_gather(gain_part, ('grp', 'z'), axis=0), axis=0)  27.3 us
    ppermute x7, waiting for transfers between devices, body(): lax.ppermute(part.astype(jnp.bfloat16), 'z', shifts(size_z, offset))  26.7 us
    all_gather x1, blocking collectives, body(): info = lax.all_gather(info, 'z', axis=0)  23.9 us
    all_to_all x3, starting transfers between devices, body(): lax.all_to_all(produced.reshape(plane_experts, slots, width_out), ('x', '...  21 us
    all_gather x1, blocking collectives, body(): gain_part = jnp.sum(lax.all_gather(gain_part, ('x', 'y'), axis=0), axis=0)  19.1 us
    all_to_all x3, starting transfers between devices, body(): lax.all_to_all(outgoing.reshape(plane_experts, slots, width_in), ('x', 'y...  18.7 us
    dot_general x3, matrix products, expert_rows(): hidden_both = jnp.dot(inputs, gate_up, preferred_element_type=jnp.float32)  17.5 us
  transfers between devices with their start and end apart: 27, of which 18 were waited for; matrix products, arithmetic and copies ran while one was open for 16% of the time, Pallas kernels for 0%

profile of v2, /device:TPU:1, one launch (start us, length us, event | category | flops | bytes accessed | tf_op | source)
XLA Modules:
  0.0 362.6 jit_solution(14278018384047817180)
XLA Ops:
  7.2 6.5 %collective-permute-start = (bf16[128,2048]{1,0:T(8,128)(2,1)}, bf16[128,2048]{1,0:T(8,128)(2,1)S(1)}, u32[]{:S(2)}, u32[]{:S(2)}) collective-permute-start(bf16[128,2048]{1,0:T(8,128)(2,1)} %param.9), channel_id=1, source_target_pairs={{0,28},{4,0},{8,4},{12,8},{16,12},{20,16},{24,20},{28,24},{1,29},{... | collective-permute-start | bytes 1572872 | tf_op jit(solution)/shard_map/ppermute | solution.py:63
  13.7 0.7 convert_bitcast_fusion
  15.0 23.9 %all-gather = f32[128,128]{1,0:T(8,128)S(1)} all-gather(f32[16,128]{1,0:T(8,128)S(1)} %pad_maximum_fusion.3), channel_id=2, replica_groups=mesh['grp'=2,'x'=4,'z'=8,'y'=4] {'z'}, dimensions={0}, use_global_device_ids=true | all-gather | bytes 73728 | tf_op jit(solution)/shard_map/all_gather | solution.py:68
  39.9 3.0 convolution_convert_fusion.3
  42.9 6.8 %all-to-all-start = ((bf16[16,24,2048]{2,1,0:T(8,128)(2,1)}), bf16[16,24,2048]{2,1,0:T(8,128)(2,1)S(1)}, u32[]{:S(2)}, u32[]{:S(2)}) async-start(bf16[16,24,2048]{2,1,0:T(8,128)(2,1)} %bitcast.10), calls=%async_computation | async-start | bytes 3145728 | tf_op jit(solution)/shard_map/all_to_all | solution.py:94
  49.7 1.9 collective-permute-start.2
  51.5 1.3 collective-permute-start.3
  52.8 6.8 %collective-permute-done.2 = bf16[128,2048]{1,0:T(8,128)(2,1)} collective-permute-done((bf16[128,2048]{1,0:T(8,128)(2,1)}, bf16[128,2048]{1,0:T(8,128)(2,1)}, u32[]{:S(2)}, u32[]{:S(2)}) %collective-permute-start.2) | collective-permute-done | bytes 524320 | tf_op jit(solution)/shard_map/ppermute | solution.py:65
  60.1 2.3 collective-permute-start.5
  62.4 2.7 all-to-all-done
  65.1 4.7 %fusion.4 = f32[384,1536]{1,0:T(8,128)S(1)} fusion(bf16[384,2048]{1,0:T(8,128)(2,1)S(1)} %bitcast.121, bf16[1,2048,1536]{2,1,0:T(8,128)(2,1)} %param.12), kind=kOutput, calls=%fused_computation.6 | convolution fusion | flops 2415919104 | bytes 10223616 | tf_op jit(solution)/shard_map/dot_general | solution.py:21
  69.8 1.7 fusion.21
  71.5 5.4 %all-to-all-start.1 = ((bf16[16,24,1024]{2,1,0:T(8,128)(2,1)}), bf16[16,24,1024]{2,1,0:T(8,128)(2,1)S(1)}, u32[]{:S(2)}, u32[]{:S(2)}) async-start(bf16[16,24,1024]{2,1,0:T(8,128)(2,1)} %bitcast.14), calls=%async_computation.1 | async-start | bytes 1572864 | tf_op jit(solution)/shard_map/all_to_all | solution.py:99
  76.9 1.8 collective-permute-start.10
  78.7 1.3 collective-permute-start.11
  80.0 6.7 %collective-permute-done.10 = bf16[128,2048]{1,0:T(8,128)(2,1)S(1)} collective-permute-done((bf16[128,2048]{1,0:T(8,128)(2,1)}, bf16[128,2048]{1,0:T(8,128)(2,1)S(1)}, u32[]{:S(2)}, u32[]{:S(2)}) %collective-permute-start.10) | collective-permute-done | bytes 524320 | tf_op jit(solution)/shard_map/ppermute | solution.py:65
  86.7 0.8 collective-permute-done.11
  87.5 1.8 convolution_convert_fusion.2
  89.2 0.9 copy-done.3
  90.1 7.2 %all-to-all-start.4 = ((bf16[16,24,2048]{2,1,0:T(8,128)(2,1)}), bf16[16,24,2048]{2,1,0:T(8,128)(2,1)S(1)}, u32[]{:S(2)}, u32[]{:S(2)}) async-start(bf16[16,24,2048]{2,1,0:T(8,128)(2,1)} %bitcast.36), calls=%async_computation.4 | async-start | bytes 3145728 | tf_op jit(solution)/shard_map/all_to_all | solution.py:94
  97.7 5.0 %convolution_convert_fusion = bf16[768,2048]{1,0:T(8,128)(2,1)} fusion(pred[768,512]{1,0:T(32,128)(4,1)S(1)} %bitcast_compare_fusion, bf16[128,2048]{1,0:T(8,128)(2,1)} %collective-permute-done.5, bf16[128,2048]{1,0:T(8,128)(2,1)} %collective-permute-done.4, bf16[128,2048]{1,0:T(8,128)(2,1)} %collective-permute-done.3, ...), kind=kOutput, calls=%fused_computation.8 | convolution fusion | flops 1620574208 | bytes 5636096 | tf_op jit(solution)/shard_map/dot_general | solution.py:93
  102.7 9.6 %all-to-all-done.4 = bf16[16,24,2048]{2,1,0:T(8,128)(2,1)S(1)} async-done(((bf16[16,24,2048]{2,1,0:T(8,128)(2,1)}), bf16[16,24,2048]{2,1,0:T(8,128)(2,1)S(1)}, u32[]{:S(2)}, u32[]{:S(2)}) %all-to-all-start.4) | async-done | bytes 1572896 | tf_op jit(solution)/shard_map/all_to_all | solution.py:94
  112.3 4.8 %all-to-all-start.2 = ((bf16[16,48,2048]{2,1,0:T(8,128)(2,1)}), bf16[16,48,2048]{2,1,0:T(8,128)(2,1)}, u32[]{:S(2)}, u32[]{:S(2)}) async-start(bf16[16,48,2048]{2,1,0:T(8,128)(2,1)} %bitcast.118), calls=%async_computation.2 | async-start | bytes 6291456 | tf_op jit(solution)/shard_map/all_to_all | solution.py:94
  118.3 1.0 scatter_custom_fusion
  119.6 4.7 %fusion = f32[384,1536]{1,0:T(8,128)S(1)} fusion(bf16[384,2048]{1,0:T(8,128)(2,1)S(1)} %bitcast.120, bf16[1,2048,1536]{2,1,0:T(8,128)(2,1)} %param.12), kind=kOutput, calls=%fused_computation.2 | convolution fusion | flops 2415919104 | bytes 10223616 | tf_op jit(solution)/shard_map/dot_general | solution.py:21
  124.3 1.7 fusion.24
  126.0 17.6 %all-to-all-done.2 = bf16[16,48,2048]{2,1,0:T(8,128)(2,1)} async-done(((bf16[16,48,2048]{2,1,0:T(8,128)(2,1)}), bf16[16,48,2048]{2,1,0:T(8,128)(2,1)}, u32[]{:S(2)}, u32[]{:S(2)}) %all-to-all-start.2) | async-done | bytes 3145760 | tf_op jit(solution)/shard_map/all_to_all | solution.py:94
  143.6 9.2 %all-to-all-start.5 = ((bf16[16,24,1024]{2,1,0:T(8,128)(2,1)}), bf16[16,24,1024]{2,1,0:T(8,128)(2,1)S(1)}, u32[]{:S(2)}, u32[]{:S(2)}) async-start(bf16[16,24,1024]{2,1,0:T(8,128)(2,1)} %bitcast.38), calls=%async_computation.5 | async-start | bytes 1572864 | tf_op jit(solution)/shard_map/all_to_all | solution.py:99
  152.8 8.1 %fusion.2 = f32[768,1536]{1,0:T(8,128)S(1)} fusion(bf16[768,2048]{1,0:T(8,128)(2,1)} %bitcast.27, bf16[1,2048,1536]{2,1,0:T(8,128)(2,1)} %param.12), kind=kOutput, calls=%fused_computation.4 | convolution fusion | flops 4831838208 | bytes 14155776 | tf_op jit(solution)/shard_map/dot_general | solution.py:21
  160.9 2.6 convolution_convert_fusion.4
  163.5 1.3 all-to-all-done.5
  164.8 6.4 %all-to-all-start.3 = ((bf16[16,48,1024]{2,1,0:T(8,128)(2,1)}), bf16[16,48,1024]{2,1,0:T(8,128)(2,1)S(1)}, u32[]{:S(2)}, u32[]{:S(2)}) async-start(bf16[16,48,1024]{2,1,0:T(8,128)(2,1)} %bitcast.28), calls=%async_computation.3 | async-start | bytes 3145728 | tf_op jit(solution)/shard_map/all_to_all | solution.py:99
  173.6 0.7 fusion.119
  174.3 8.2 %collective-permute-start.13 = (bf16[128,1024]{1,0:T(8,128)(2,1)}, bf16[128,1024]{1,0:T(8,128)(2,1)S(1)}, u32[]{:S(2)}, u32[]{:S(2)}) collective-permute-start(bf16[128,1024]{1,0:T(8,128)(2,1)} %get-tuple-element.15), channel_id=1, source_target_pairs={{0,16},{4,20},{8,24},{12,28},{16,0},{20,4},{24,8},{28,12},{1,17},{... | collective-permute-start | bytes 786440 | tf_op jit(solution)/shard_map/ppermute | solution.py:115
  183.1 7.4 %all-to-all-done.3 = bf16[16,48,1024]{2,1,0:T(8,128)(2,1)S(1)} async-done(((bf16[16,48,1024]{2,1,0:T(8,128)(2,1)}), bf16[16,48,1024]{2,1,0:T(8,128)(2,1)S(1)}, u32[]{:S(2)}, u32[]{:S(2)}) %all-to-all-start.3) | async-done | bytes 1572896 | tf_op jit(solution)/shard_map/all_to_all | solution.py:99
  190.5 1.0 fusion.44
  191.5 1.0 fusion.14
  192.6 3.7 %collective-permute-start.9 = (bf16[128,1024]{1,0:T(8,128)(2,1)S(1)}, bf16[128,1024]{1,0:T(8,128)(2,1)S(1)}, u32[]{:S(2)}, u32[]{:S(2)}) collective-permute-start(bf16[128,1024]{1,0:T(8,128)(2,1)S(1)} %get-tuple-element.9), channel_id=1, source_target_pairs={{0,12},{4,16},{8,20},{12,24},{16,28},{20,0},{24,4},{28,8},{1,13},{... | collective-permute-start | bytes 786440 | tf_op jit(solution)/shard_map/ppermute | solution.py:115
  196.9 1.9 collective-permute-start.7
  198.7 0.9 collective-permute-start.6
  199.8 7.6 %collective-permute-done.9 = bf16[128,1024]{1,0:T(8,128)(2,1)S(1)} collective-permute-done((bf16[128,1024]{1,0:T(8,128)(2,1)S(1)}, bf16[128,1024]{1,0:T(8,128)(2,1)S(1)}, u32[]{:S(2)}, u32[]{:S(2)}) %collective-permute-start.9) | collective-permute-done | bytes 262176 | tf_op jit(solution)/shard_map/ppermute | solution.py:115
  207.5 8.9 %collective-permute-done.8 = bf16[128,1024]{1,0:T(8,128)(2,1)S(1)} collective-permute-done((bf16[128,1024]{1,0:T(8,128)(2,1)S(1)}, bf16[128,1024]{1,0:T(8,128)(2,1)S(1)}, u32[]{:S(2)}, u32[]{:S(2)}) %collective-permute-start.8) | collective-permute-done | bytes 262176 | tf_op jit(solution)/shard_map/ppermute | solution.py:115
  216.4 6.0 %collective-permute-done.7 = bf16[128,1024]{1,0:T(8,128)(2,1)S(1)} collective-permute-done((bf16[128,1024]{1,0:T(8,128)(2,1)S(1)}, bf16[128,1024]{1,0:T(8,128)(2,1)S(1)}, u32[]{:S(2)}, u32[]{:S(2)}) %collective-permute-start.7) | collective-permute-done | bytes 262176 | tf_op jit(solution)/shard_map/ppermute | solution.py:115
  222.4 4.1 %collective-permute-done.6 = bf16[128,1024]{1,0:T(8,128)(2,1)S(1)} collective-permute-done((bf16[128,1024]{1,0:T(8,128)(2,1)S(1)}, bf16[128,1024]{1,0:T(8,128)(2,1)S(1)}, u32[]{:S(2)}, u32[]{:S(2)}) %collective-permute-start.6) | collective-permute-done | bytes 262176 | tf_op jit(solution)/shard_map/ppermute | solution.py:115
  227.1 0.9 gather_fusion
  228.4 0.8 reduce.2
  229.2 0.9 reshape.224
  230.1 13.0 %all-to-all-start.6 = ((bf16[128,2,512]{2,1,0:T(2,128)(2,1)}), bf16[128,2,512]{2,1,0:T(2,128)(2,1)S(1)}, u32[]{:S(2)}, u32[]{:S(2)}) async-start(bf16[128,2,512]{2,1,0:T(2,128)(2,1)} %reshape.224), calls=%async_computation.6 | async-start | bytes 524288 | tf_op jit(solution)/shard_map/all_to_all | solution.py:126
  243.7 7.7 %collective-permute-start.14 = (bf16[128,1792]{0,1:T(8,128)(2,1)S(1)}, bf16[128,1792]{0,1:T(8,128)(2,1)S(1)}, u32[]{:S(2)}, u32[]{:S(2)}) collective-permute-start(bf16[128,1792]{0,1:T(8,128)(2,1)S(1)} %bitcast.123), channel_id=1, source_target_pairs={{0,128},{128,0},{1,129},{129,1},{2,130},{130,2},{3,131},{131,3},{4... | collective-permute-start | bytes 1376264 | tf_op jit(solution)/shard_map/ppermute | solution.py:141
  251.4 5.5 %all-to-all-done.6 = bf16[128,2,512]{2,1,0:T(2,128)(2,1)S(1)} async-done(((bf16[128,2,512]{2,1,0:T(2,128)(2,1)}), bf16[128,2,512]{2,1,0:T(2,128)(2,1)S(1)}, u32[]{:S(2)}, u32[]{:S(2)}) %all-to-all-start.6) | async-done | bytes 262176 | tf_op jit(solution)/shard_map/all_to_all | solution.py:126
  257.1 10.3 %all-gather.8.cloned.1.call-done = bf16[128,14,1024]{2,1,0:T(8,128)(2,1)} async-done(((bf16[1,14,1024]{2,1,0:T(8,128)(2,1)}), bf16[128,14,1024]{2,1,0:T(8,128)(2,1)}) %all-gather.8.cloned.1.call-update) | async-done | bytes 3670032 | tf_op jit(solution)/shard_map/all_gather | solution.py:129
  267.4 6.4 %reshape.208 = bf16[1792,1024]{1,0:T(8,128)(2,1)} reshape(bf16[128,14,1024]{2,1,0:T(8,128)(2,1)} %all-gather.8.cloned.1.call-done) | data formatting | bytes 7340032
  273.8 2.8 fusion.118
  276.7 4.0 %collective-permute-start.15 = (bf16[128,512]{1,0:T(8,128)(2,1)S(1)}, bf16[128,512]{1,0:T(8,128)(2,1)S(1)}, u32[]{:S(2)}, u32[]{:S(2)}) collective-permute-start(bf16[128,512]{1,0:T(8,128)(2,1)S(1)} %get-tuple-element.17), channel_id=1, source_target_pairs={{0,128},{128,0},{1,129},{129,1},{2,130},{130,2},{3,131},{131,3},{4... | collective-permute-start | bytes 393224 | tf_op jit(solution)/shard_map/ppermute | solution.py:150
  280.7 1.0 collective-permute-done.15
  281.7 1.9 convolution_convert_fusion.1
  283.6 3.6 %fusion.50 = (f32[1792]{0:T(1024)S(1)}, f32[128]{0:T(128)S(1)}, f32[128,1792]{1,0:T(8,128)S(1)}) fusion(bf16[128,1792]{1,0:T(8,128)(2,1)S(1)} %copy-done.2, f32[128]{0:T(128)S(1)} %add_rsqrt_fusion.1, f32[1792]{0:T(1024)S(1)} %copy-done.8, bf16[128,1024]{1,0:T(8,128)(2,1)S(1)} %get-tuple-element.12, bf16[1792,1024]{1,0:T(8,128)(2,1)} %reshape.208), kind=kOutput, calls=%fused_computation.68 | convolution fusion | flops 471365760 | bytes 5323776 | tf_op jit(solution)/shard_map/dot_general | solution.py:166
  287.3 27.3 %all-gather.4 = f32[16,1,1792]{2,1,0:T(1,128)S(1)} all-gather(f32[1,1,1792]{2,1,0:T(1,128)S(1)} %reshape.209), channel_id=3, replica_groups=mesh['grp'=2,'x'=4,'z'=8,'y'=4] {'grp','z'}, dimensions={0}, use_global_device_ids=true | all-gather | bytes 121856 | tf_op jit(solution)/shard_map/all_gather | solution.py:175
  314.7 19.1 %all-gather.5 = f32[16,1,1792]{2,1,0:T(1,128)S(1)} all-gather(f32[1,1,1792]{2,1,0:T(1,128)S(1)} %reshape.211), channel_id=4, replica_groups=mesh['grp'=2,'x'=4,'z'=8,'y'=4] {'x','y'}, dimensions={0}, use_global_device_ids=true | all-gather | bytes 121856 | tf_op jit(solution)/shard_map/all_gather | solution.py:176
  333.8 1.1 fusion.49
  334.9 1.7 reshape.184
  336.6 3.9 %all-to-all-start.7 = ((bf16[16,14,512]{2,1,0:T(8,128)(2,1)}), bf16[16,14,512]{2,1,0:T(8,128)(2,1)S(1)}, u32[]{:S(2)}, u32[]{:S(2)}) async-start(bf16[16,14,512]{2,1,0:T(8,128)(2,1)} %reshape.184), calls=%async_computation.8 | async-start | bytes 524288 | tf_op jit(solution)/shard_map/all_to_all | solution.py:156
  341.1 6.7 %all-to-all-done.7 = bf16[16,14,512]{2,1,0:T(8,128)(2,1)S(1)} async-done(((bf16[16,14,512]{2,1,0:T(8,128)(2,1)}), bf16[16,14,512]{2,1,0:T(8,128)(2,1)S(1)}, u32[]{:S(2)}, u32[]{:S(2)}) %all-to-all-start.7) | async-done | bytes 229408 | tf_op jit(solution)/shard_map/all_to_all | solution.py:156
  347.9 6.4 %collective-permute-start.16 = (f32[14,512]{1,0:T(8,128)S(1)}, f32[14,512]{1,0:T(8,128)S(1)}, u32[]{:S(2)}, u32[]{:S(2)}) collective-permute-start(f32[14,512]{1,0:T(8,128)S(1)} %broadcast_multiply_fusion), channel_id=1, source_target_pairs={{0,128},{128,0},{1,129},{129,1},{2,130},{130,2},{3,131},{131,3},{4... | collective-permute-start | bytes 86024 | tf_op jit(solution)/shard_map/ppermute | solution.py:160
  (95 shorter events, 11.7 us)
Async XLA Ops:
  7.2 62.6 %copy-start = (bf16[1,768,1024]{2,1,0:T(8,128)(2,1)S(1)}, bf16[1,768,1024]{2,1,0:T(8,128)(2,1)}, u32[]{:S(2)}) copy-start(bf16[1,768,1024]{2,1,0:T(8,128)(2,1)} %param.13) | copy-start | bytes 4718596
  7.2 32.7 %collective-permute-start = (bf16[128,2048]{1,0:T(8,128)(2,1)}, bf16[128,2048]{1,0:T(8,128)(2,1)S(1)}, u32[]{:S(2)}, u32[]{:S(2)}) collective-permute-start(bf16[128,2048]{1,0:T(8,128)(2,1)} %param.9), channel_id=1, source_target_pairs={{0,28},{4,0},{8,4},{12,8},{16,12},{20,16},{24,20},{28,24},{1,29},{... | collective-permute-start | bytes 1572872 | tf_op jit(solution)/shard_map/ppermute | solution.py:63
  39.9 3.0 copy-start.7
  42.9 22.2 %all-to-all-start = ((bf16[16,24,2048]{2,1,0:T(8,128)(2,1)}), bf16[16,24,2048]{2,1,0:T(8,128)(2,1)S(1)}, u32[]{:S(2)}, u32[]{:S(2)}) async-start(bf16[16,24,2048]{2,1,0:T(8,128)(2,1)} %bitcast.10), calls=%async_computation | async-start | bytes 3145728 | tf_op jit(solution)/shard_map/all_to_all | solution.py:94
  49.7 10.0 %collective-permute-start.2 = (bf16[128,2048]{1,0:T(8,128)(2,1)}, bf16[128,2048]{1,0:T(8,128)(2,1)}, u32[]{:S(2)}, u32[]{:S(2)}) collective-permute-start(bf16[128,2048]{1,0:T(8,128)(2,1)} %param.9), channel_id=1, source_target_pairs={{0,4},{4,8},{8,12},{12,16},{16,20},{20,24},{24,28},{28,0},{1,5},{5... | collective-permute-start | bytes 1572872 | tf_op jit(solution)/shard_map/ppermute | solution.py:65
  51.5 8.5 %collective-permute-start.3 = (bf16[128,2048]{1,0:T(8,128)(2,1)}, bf16[128,2048]{1,0:T(8,128)(2,1)}, u32[]{:S(2)}, u32[]{:S(2)}) collective-permute-start(bf16[128,2048]{1,0:T(8,128)(2,1)} %copy-done.7), channel_id=1, source_target_pairs={{0,28},{4,0},{8,4},{12,8},{16,12},{20,16},{24,20},{28,24},{1,29},{... | collective-permute-start | bytes 1572872 | tf_op jit(solution)/shard_map/ppermute | solution.py:63
  59.6 17.3 %collective-permute-start.4 = (bf16[128,2048]{1,0:T(8,128)(2,1)}, bf16[128,2048]{1,0:T(8,128)(2,1)}, u32[]{:S(2)}, u32[]{:S(2)}) collective-permute-start(bf16[128,2048]{1,0:T(8,128)(2,1)} %collective-permute-done.2), channel_id=1, source_target_pairs={{0,4},{4,8},{8,12},{12,16},{16,20},{20,24},{24,28},{28,0},{1,5},{5... | collective-permute-start | bytes 1572872 | tf_op jit(solution)/shard_map/ppermute | solution.py:65
  60.1 18.6 %collective-permute-start.5 = (bf16[128,2048]{1,0:T(8,128)(2,1)}, bf16[128,2048]{1,0:T(8,128)(2,1)}, u32[]{:S(2)}, u32[]{:S(2)}) collective-permute-start(bf16[128,2048]{1,0:T(8,128)(2,1)} %collective-permute-done.3), channel_id=1, source_target_pairs={{0,28},{4,0},{8,4},{12,8},{16,12},{20,16},{24,20},{28,24},{1,29},{... | collective-permute-start | bytes 1572872 | tf_op jit(solution)/shard_map/ppermute | solution.py:63
  71.5 17.7 %all-to-all-start.1 = ((bf16[16,24,1024]{2,1,0:T(8,128)(2,1)}), bf16[16,24,1024]{2,1,0:T(8,128)(2,1)S(1)}, u32[]{:S(2)}, u32[]{:S(2)}) async-start(bf16[16,24,1024]{2,1,0:T(8,128)(2,1)} %bitcast.14), calls=%async_computation.1 | async-start | bytes 1572864 | tf_op jit(solution)/shard_map/all_to_all | solution.py:99
  76.9 9.8 %collective-permute-start.10 = (bf16[128,2048]{1,0:T(8,128)(2,1)}, bf16[128,2048]{1,0:T(8,128)(2,1)S(1)}, u32[]{:S(2)}, u32[]{:S(2)}) collective-permute-start(bf16[128,2048]{1,0:T(8,128)(2,1)} %collective-permute-done.4), channel_id=1, source_target_pairs={{0,4},{4,8},{8,12},{12,16},{16,20},{20,24},{24,28},{28,0},{1,5},{5... | collective-permute-start | bytes 1572872 | tf_op jit(solution)/shard_map/ppermute | solution.py:65
  78.7 8.8 %collective-permute-start.11 = (bf16[128,2048]{1,0:T(8,128)(2,1)}, bf16[128,2048]{1,0:T(8,128)(2,1)S(1)}, u32[]{:S(2)}, u32[]{:S(2)}) collective-permute-start(bf16[128,2048]{1,0:T(8,128)(2,1)} %collective-permute-done.5), channel_id=1, source_target_pairs={{0,28},{4,0},{8,4},{12,8},{16,12},{20,16},{24,20},{28,24},{1,29},{... | collective-permute-start | bytes 1572872 | tf_op jit(solution)/shard_map/ppermute | solution.py:63
  89.2 0.9 copy-start.3
  90.1 22.2 %all-to-all-start.4 = ((bf16[16,24,2048]{2,1,0:T(8,128)(2,1)}), bf16[16,24,2048]{2,1,0:T(8,128)(2,1)S(1)}, u32[]{:S(2)}, u32[]{:S(2)}) async-start(bf16[16,24,2048]{2,1,0:T(8,128)(2,1)} %bitcast.36), calls=%async_computation.4 | async-start | bytes 3145728 | tf_op jit(solution)/shard_map/all_to_all | solution.py:94
  112.3 5.5 %copy-start.9 = (s32[128]{0:T(128)S(1)}, s32[128]{0:T(128)}, u32[]{:S(2)}) copy-start(s32[128]{0:T(128)} %param.14) | copy-start | bytes 1540
  112.3 31.3 %all-to-all-start.2 = ((bf16[16,48,2048]{2,1,0:T(8,128)(2,1)}), bf16[16,48,2048]{2,1,0:T(8,128)(2,1)}, u32[]{:S(2)}, u32[]{:S(2)}) async-start(bf16[16,48,2048]{2,1,0:T(8,128)(2,1)} %bitcast.118), calls=%async_computation.2 | async-start | bytes 6291456 | tf_op jit(solution)/shard_map/all_to_all | solution.py:94
  117.1 150.3 %all-gather.8.cloned.1.call-start = ((), (), s32[]{:S(2)}) async-start(), calls=%async_computation.10 | async-start | bytes 4227072 | tf_op jit(solution)/shard_map/all_gather | solution.py:129
  143.6 21.2 %all-to-all-start.5 = ((bf16[16,24,1024]{2,1,0:T(8,128)(2,1)}), bf16[16,24,1024]{2,1,0:T(8,128)(2,1)S(1)}, u32[]{:S(2)}, u32[]{:S(2)}) async-start(bf16[16,24,1024]{2,1,0:T(8,128)(2,1)} %bitcast.38), calls=%async_computation.5 | async-start | bytes 1572864 | tf_op jit(solution)/shard_map/all_to_all | solution.py:99
  163.5 7.7 %copy-start.4 = (bf16[16,24,1024]{2,1,0:T(8,128)(2,1)S(1)}, bf16[16,24,1024]{2,1,0:T(8,128)(2,1)}, u32[]{:S(2)}) copy-start(bf16[16,24,1024]{2,1,0:T(8,128)(2,1)} %copy-done.3) | copy-start | bytes 2359300
  164.8 25.7 %all-to-all-start.3 = ((bf16[16,48,1024]{2,1,0:T(8,128)(2,1)}), bf16[16,48,1024]{2,1,0:T(8,128)(2,1)S(1)}, u32[]{:S(2)}, u32[]{:S(2)}) async-start(bf16[16,48,1024]{2,1,0:T(8,128)(2,1)} %bitcast.28), calls=%async_computation.3 | async-start | bytes 3145728 | tf_op jit(solution)/shard_map/all_to_all | solution.py:99
  172.1 1.0 copy-start.5
  172.2 24.7 %collective-permute-start.1 = (bf16[128,1024]{1,0:T(8,128)(2,1)S(1)}, bf16[128,1024]{1,0:T(8,128)(2,1)S(1)}, u32[]{:S(2)}, u32[]{:S(2)}) collective-permute-start(bf16[128,1024]{1,0:T(8,128)(2,1)S(1)} %slice.241), channel_id=1, source_target_pairs={{0,4},{4,8},{8,12},{12,16},{16,20},{20,24},{24,28},{28,0},{1,5},{5... | collective-permute-start | bytes 786440 | tf_op jit(solution)/shard_map/ppermute | solution.py:115
  174.3 24.4 %collective-permute-start.13 = (bf16[128,1024]{1,0:T(8,128)(2,1)}, bf16[128,1024]{1,0:T(8,128)(2,1)S(1)}, u32[]{:S(2)}, u32[]{:S(2)}) collective-permute-start(bf16[128,1024]{1,0:T(8,128)(2,1)} %get-tuple-element.15), channel_id=1, source_target_pairs={{0,16},{4,20},{8,24},{12,28},{16,0},{20,4},{24,8},{28,12},{1,17},{... | collective-permute-start | bytes 786440 | tf_op jit(solution)/shard_map/ppermute | solution.py:115
  182.5 17.3 %collective-permute-start.12 = (bf16[128,1024]{1,0:T(8,128)(2,1)S(1)}, bf16[128,1024]{1,0:T(8,128)(2,1)S(1)}, u32[]{:S(2)}, u32[]{:S(2)}) collective-permute-start(bf16[128,1024]{1,0:T(8,128)(2,1)S(1)} %get-tuple-element.14), channel_id=1, source_target_pairs={{0,20},{4,24},{8,28},{12,0},{16,4},{20,8},{24,12},{28,16},{1,21},{... | collective-permute-start | bytes 786440 | tf_op jit(solution)/shard_map/ppermute | solution.py:115
  192.5 7.1 %copy-start.2 = (bf16[128,1792]{1,0:T(8,128)(2,1)S(1)}, bf16[128,1792]{1,0:T(8,128)(2,1)}, u32[]{:S(2)}) copy-start(bf16[128,1792]{1,0:T(8,128)(2,1)} %param.15) | copy-start | bytes 1376260
  192.5 34.0 %copy-start.6 = (f32[256,1024]{1,0:T(8,128)S(1)}, f32[256,1024]{1,0:T(8,128)}, u32[]{:S(2)}) copy-start(f32[256,1024]{1,0:T(8,128)} %copy-done.5) | copy-start | bytes 3145732
  192.6 14.9 %collective-permute-start.9 = (bf16[128,1024]{1,0:T(8,128)(2,1)S(1)}, bf16[128,1024]{1,0:T(8,128)(2,1)S(1)}, u32[]{:S(2)}, u32[]{:S(2)}) collective-permute-start(bf16[128,1024]{1,0:T(8,128)(2,1)S(1)} %get-tuple-element.9), channel_id=1, source_target_pairs={{0,12},{4,16},{8,20},{12,24},{16,28},{20,0},{24,4},{28,8},{1,13},{... | collective-permute-start | bytes 786440 | tf_op jit(solution)/shard_map/ppermute | solution.py:115
  196.4 20.0 %collective-permute-start.8 = (bf16[128,1024]{1,0:T(8,128)(2,1)S(1)}, bf16[128,1024]{1,0:T(8,128)(2,1)S(1)}, u32[]{:S(2)}, u32[]{:S(2)}) collective-permute-start(bf16[128,1024]{1,0:T(8,128)(2,1)S(1)} %get-tuple-element.10), channel_id=1, source_target_pairs={{0,24},{4,28},{8,0},{12,4},{16,8},{20,12},{24,16},{28,20},{1,25},{... | collective-permute-start | bytes 786440 | tf_op jit(solution)/shard_map/ppermute | solution.py:115
  196.9 25.5 %collective-permute-start.7 = (bf16[128,1024]{1,0:T(8,128)(2,1)S(1)}, bf16[128,1024]{1,0:T(8,128)(2,1)S(1)}, u32[]{:S(2)}, u32[]{:S(2)}) collective-permute-start(bf16[128,1024]{1,0:T(8,128)(2,1)S(1)} %get-tuple-element.11), channel_id=1, source_target_pairs={{0,8},{4,12},{8,16},{12,20},{16,24},{20,28},{24,0},{28,4},{1,9},{5... | collective-permute-start | bytes 786440 | tf_op jit(solution)/shard_map/ppermute | solution.py:115
  198.7 27.8 %collective-permute-start.6 = (bf16[128,1024]{1,0:T(8,128)(2,1)S(1)}, bf16[128,1024]{1,0:T(8,128)(2,1)S(1)}, u32[]{:S(2)}, u32[]{:S(2)}) collective-permute-start(bf16[128,1024]{1,0:T(8,128)(2,1)S(1)} %get-tuple-element.8), channel_id=1, source_target_pairs={{0,28},{4,0},{8,4},{12,8},{16,12},{20,16},{24,20},{28,24},{1,29},{... | collective-permute-start | bytes 786440 | tf_op jit(solution)/shard_map/ppermute | solution.py:115
  227.1 16.1 %copy-start.8 = (f32[1792]{0:T(1024)S(1)}, f32[1792]{0:T(1024)}, u32[]{:S(2)}) copy-start(f32[1792]{0:T(1024)} %param.16) | copy-start | bytes 21508
  230.1 26.8 %all-to-all-start.6 = ((bf16[128,2,512]{2,1,0:T(2,128)(2,1)}), bf16[128,2,512]{2,1,0:T(2,128)(2,1)S(1)}, u32[]{:S(2)}, u32[]{:S(2)}) async-start(bf16[128,2,512]{2,1,0:T(2,128)(2,1)} %reshape.224), calls=%async_computation.6 | async-start | bytes 524288 | tf_op jit(solution)/shard_map/all_to_all | solution.py:126
  243.1 91.8 %reduce-scatter.2.cloned.1.call-start = ((), (), s32[]{:S(2)}) async-start(), calls=%async_computation.9 | async-start | bytes 2064384 | tf_op jit(solution)/shard_map/reduce_scatter | solution.py:154
  243.7 37.0 %collective-permute-start.14 = (bf16[128,1792]{0,1:T(8,128)(2,1)S(1)}, bf16[128,1792]{0,1:T(8,128)(2,1)S(1)}, u32[]{:S(2)}, u32[]{:S(2)}) collective-permute-start(bf16[128,1792]{0,1:T(8,128)(2,1)S(1)} %bitcast.123), channel_id=1, source_target_pairs={{0,128},{128,0},{1,129},{129,1},{2,130},{130,2},{3,131},{131,3},{4... | collective-permute-start | bytes 1376264 | tf_op jit(solution)/shard_map/ppermute | solution.py:141
  276.7 5.0 %collective-permute-start.15 = (bf16[128,512]{1,0:T(8,128)(2,1)S(1)}, bf16[128,512]{1,0:T(8,128)(2,1)S(1)}, u32[]{:S(2)}, u32[]{:S(2)}) collective-permute-start(bf16[128,512]{1,0:T(8,128)(2,1)S(1)} %get-tuple-element.17), channel_id=1, source_target_pairs={{0,128},{128,0},{1,129},{129,1},{2,130},{130,2},{3,131},{131,3},{4... | collective-permute-start | bytes 393224 | tf_op jit(solution)/shard_map/ppermute | solution.py:150
  283.6 72.2 %copy-start.1 = (bf16[1,768,1024]{2,1,0:T(8,128)(2,1)S(1)}, bf16[1,768,1024]{2,1,0:T(8,128)(2,1)}, u32[]{:S(2)}) copy-start(bf16[1,768,1024]{2,1,0:T(8,128)(2,1)} %param.13) | copy-start | bytes 4718596
  336.6 11.2 %all-to-all-start.7 = ((bf16[16,14,512]{2,1,0:T(8,128)(2,1)}), bf16[16,14,512]{2,1,0:T(8,128)(2,1)S(1)}, u32[]{:S(2)}, u32[]{:S(2)}) async-start(bf16[16,14,512]{2,1,0:T(8,128)(2,1)} %reshape.184), calls=%async_computation.8 | async-start | bytes 524288 | tf_op jit(solution)/shard_map/all_to_all | solution.py:156
  347.9 7.2 %collective-permute-start.16 = (f32[14,512]{1,0:T(8,128)S(1)}, f32[14,512]{1,0:T(8,128)S(1)}, u32[]{:S(2)}, u32[]{:S(2)}) collective-permute-start(f32[14,512]{1,0:T(8,128)S(1)} %broadcast_multiply_fusion), channel_id=1, source_target_pairs={{0,128},{128,0},{1,129},{129,1},{2,130},{130,2},{3,131},{131,3},{4... | collective-permute-start | bytes 86024 | tf_op jit(solution)/shard_map/ppermute | solution.py:160
Sparse Core Ops, SparseCore 0:
  121.6 145.7 all-gather.7
  283.7 34.8 reduce-scatter.1
